TPU v7x, 256 devices: a whole 4x4x8 slice. The times are simulated.
256 devices in a mesh: face: 4 (over z_lo, core), tile: 64 (over y, z_hi, x).
Axes of the slice: x: 4, y: 4, z: 8 (z_hi: 4, z_lo: 2; z = z_hi * 2 + z_lo), core: 2. Of those that a mesh axis runs over, the one named last changes fastest.
Arguments:
- pressure: float32 [64, 4096, 256], P(None, ('face', 'tile')), may hold values from -0.8 to 0.8
- forcing: float32 [64, 4096, 256], P(None, ('face', 'tile')), may hold values from -8 to 8
- stiffness: float32 [64, 4096, 256], P(None, ('face', 'tile')), may hold values from 2 to 8
- vertical_op: float32 [64, 64], replicated, as said below
- col_inverse: float32 [4, 64, 64], replicated, as said below
Outputs:
- updated: float32 [64, 4096, 256], P(None, ('face', 'tile'))
- new_residual: float32 [64, 4096, 256], P(None, ('face', 'tile'))
Inputs may be any that keep to these rules, and one draw needn't show every extreme that they name: vertical_op is symmetric positive definite. col_inverse[l] is the float32 inverse of (0.02 + 16 / 4^l) I + vertical_op.
All inputs are finite; a program needn't handle non-finite values.
Results may differ from a plain program's by a relative error of at most 0.0003.
Values sent between devices are 32-bit elements; how exact they have to be, the bound alone decides.
A program may use at most 128 MiB of HBM per device.

v0:
```python
import functools

import jax
import jax.numpy as jnp
from jax import lax
from jax.experimental import pallas as pl
from jax.experimental.pallas import tpu as pltpu
from jax.sharding import PartitionSpec as P

LEVELS = 4
LEV = 64
damping = 0.02
relax_weight = 0.6
nominal_stiff = 16.0
F32, BF16 = jnp.float32, jnp.bfloat16
MESH = pl.DeviceIdType.MESH
LANES = 128

HALO = (4, 4, 4, 5)

MESSAGES = (
    "p", "k", "r", "k_far", "k1", "k2", "k3", "k3_2", "k3_3", "d", "b1", "r0", "b2", "r1", "c1",
    "b3", "b3_2", "b3_3", "r2", "c2",
)


def split(x):
    high = x.astype(BF16)
    return high, (x - high.astype(F32)).astype(BF16)


def rows(lo, hi, step, fn):
    whole, rest = divmod(hi - lo, step)
    if whole > 1:
        def body(i, carry):
            base = lo + i * step
            fn([base + j for j in range(step)])
            return carry
        lax.fori_loop(0, whole, body, 0)
    elif whole == 1:
        fn([lo + j for j in range(step)])
    if rest:
        fn([hi - rest + j for j in range(rest)])


def lateral(x, masked):
    width = x.shape[1]
    below, above = pltpu.roll(x, 1, 1), pltpu.roll(x, width - 1, 1)
    if masked:
        lane = lax.broadcasted_iota(jnp.int32, x.shape, 1)
        below = jnp.where(lane == 0, 0.0, below)
        above = jnp.where(lane == width - 1, 0.0, above)
    return below + above


def kernel(
    faces, tiles, p_hbm, f_hbm, k_hbm, vop_ref, inv_ref, out_u, out_r,
    p0, k0, s0, r0, da0, db0, e0, v0, ph, rh, dh, lr0,
    k1, s1, r1, da1, db1, c1, e1, v1, lr1, lc1,
    k2, s2, r2, da2, db2, c2, e2, v2, lr2, lc2,
    k3, s3, r3, da3, db3, c3, v3, c0,
    w_ref, wv_ref, coarse_ref, coarse0_ref, fine_ref, fine0_ref,
    in_sem, out_sem, send_sem, recv_sem,
):
    count = faces * tiles
    me = lax.axis_index("face") * tiles + lax.axis_index("tile")

    def device(offset):
        other = lax.rem(me + (offset + count), count)
        return (other // tiles, lax.rem(other, tiles))

    barrier = pltpu.get_barrier_semaphore()
    for offset in (-3, -2, -1, 1, 2, 3):
        pl.semaphore_signal(barrier, inc=1, device_id=device(offset), device_id_type=MESH)

    K, S, R, DA, DB = (k0, k1, k2, k3), (s0, s1, s2, s3), (r0, r1, r2, r3), (da0, da1, da2, da3), (db0, db1, db2, db3)
    C = (c0, c1, c2, c3)
    own = tuple(n_rows >> level for level, n_rows in enumerate((16,) * LEVELS))
    H = HALO

    for i in range(16):
        pltpu.make_async_copy(p_hbm.at[:, i, :], p0.at[1 + i], in_sem.at[0]).start()
    for i in range(16):
        pltpu.make_async_copy(k_hbm.at[:, i, :], k0.at[H[0] + i], in_sem.at[1]).start()
    for i in range(16):
        pltpu.make_async_copy(f_hbm.at[:, i, :], r0.at[H[0] + i], in_sem.at[2]).start()

    def beside(m):
        high, low = split(m)
        return jnp.concatenate([high, high, low], axis=1)

    for level in range(LEVELS):
        w_ref[level] = beside(inv_ref[level])
    row, col = (lax.broadcasted_iota(jnp.int32, (LEV, LEV), a) for a in (0, 1))
    wv_ref[...] = beside(vop_ref[...] + jnp.where(row == col, damping, 0.0))

    def pairs(n_in, n_out, fold):
        a, b = (lax.broadcasted_iota(jnp.int32, (2 * n_in, n_out), x) for x in (0, 1))
        a = jnp.where(a >= n_in, a - n_in, a)
        hit = (a // 2 == b) if fold else (a == b // 2)
        return jnp.where(hit, 1.0, 0.0).astype(BF16)

    coarse0_ref[...] = pairs(256, 128, True)
    coarse_ref[...] = pairs(128, 128, True)
    fine0_ref[...] = pairs(128, 256, False)
    fine_ref[...] = pairs(128, 128, False)

    def stacked(x):
        high, low = split(x)
        return jnp.concatenate([high, low, high], axis=0)

    def columns(w, x):
        return jnp.dot(w, stacked(x), preferred_element_type=F32)

    def lanes(x, matrix):
        high, low = split(x)
        return jnp.dot(jnp.concatenate([high, low], axis=1), matrix, preferred_element_type=F32)

    def masked(level):
        return level < 2

    def send(name, src, dst, offset, side):
        at = MESSAGES.index(name)
        return pltpu.make_async_remote_copy(
            src_ref=src, dst_ref=dst, send_sem=send_sem.at[at, side], recv_sem=recv_sem.at[at, side],
            device_id=device(offset), device_id_type=MESH,
        )

    pending = {}

    def exchange(name, src_low, dst_low, src_high, dst_high, distance=1):
        copies = (
            send(name, src_low, dst_high, -distance, 0),
            send(name, src_high, dst_low, distance, 1),
        )
        for copy in copies:
            copy.start()
        pending[name] = copies

    def arrived(*names):
        for name in names:
            for copy in pending[name]:
                copy.wait_recv()

    def sent(*names):
        for name in names:
            for copy in pending.pop(name):
                copy.wait_send()

    def scales(level, lo, hi):
        top = relax_weight * (damping + nominal_stiff / 4.0**level)
        def fn(at):
            for i in at:
                S[level][i] = top / (damping + 4.0 * K[level][i])
        rows(lo, hi, 2, fn)

    def relax(level, lo, hi, d_ref):
        def fn(at):
            for i in at:
                d_ref[i] = columns(w_ref[level], S[level][i] * R[level][i])
        rows(lo, hi, 4, fn)

    def update(level, lo, hi, d_ref):
        shift = nominal_stiff / 4.0**level
        def fn(at):
            for i in at:
                d = d_ref[i]
                beside_sum = d_ref[i - 1] + d_ref[i + 1] + lateral(d, masked(level))
                t = S[level][i] * R[level][i]
                R[level][i] = R[level][i] - t + shift * d + K[level][i] * (beside_sum - 4.0 * d)
        rows(lo, hi, 2, fn)

    def lift(level, lo, hi, e_ref, v_ref):
        def fn(at):
            for i in at:
                e = e_ref[i]
                beside_sum = e_ref[i - 1] + e_ref[i + 1] + lateral(e, masked(level))
                R[level][i] = R[level][i] - v_ref[i] + K[level][i] * (beside_sum - 4.0 * e)
        rows(lo, hi, 2, fn)

    def coarsen(level, src, dst, scale):
        matrix = coarse0_ref if level == 0 else coarse_ref
        def fn(at):
            for j in at:
                fine = H[level] + 2 * j
                dst[H[level + 1] + j] = lanes(scale * (src[fine] + src[fine + 1]), matrix[...])
        rows(0, own[level + 1], 2, fn)

    def refine(level, lo, hi, src, e_ref, v_ref):
        matrix = fine0_ref if level == 0 else fine_ref
        def fn(at):
            for j in at:
                e = src[j]
                to = H[level] + 2 * (j - H[level + 1])
                value = lanes(e, matrix[...])
                product = lanes(columns(wv_ref[...], e), matrix[...])
                for i in (to, to + 1):
                    e_ref[i] = value
                    v_ref[i] = product
        rows(lo, hi, 2, fn)

    zero = jnp.zeros((LEV, 256), F32)
    p0[0] = zero
    p0[17] = zero
    pltpu.make_async_copy(p0.at[pl.ds(1, 16)], p0.at[pl.ds(1, 16)], in_sem.at[0]).wait()
    pltpu.make_async_copy(k0.at[pl.ds(4, 16)], k0.at[pl.ds(4, 16)], in_sem.at[1]).wait()
    pltpu.make_async_copy(r0.at[pl.ds(4, 16)], r0.at[pl.ds(4, 16)], in_sem.at[2]).wait()

    def start(at):
        for i in at:
            x = p0[i + 1]
            beside_sum = p0[i] + p0[i + 2] + lateral(x, True)
            r0[i + 4] = r0[i + 4] - columns(wv_ref[...], x) + k0[i + 4] * (beside_sum - 4.0 * x)
    rows(0, 16, 2, start)
    dh[2] = r0[4]
    dh[3] = r0[19]

    pl.semaphore_wait(barrier, 6)
    exchange("p", p0.at[1], ph.at[0], p0.at[16], ph.at[1])
    exchange("k", k0.at[4], k0.at[3], k0.at[19], k0.at[20])
    exchange("r", dh.at[2], rh.at[0], dh.at[3], rh.at[1])
    exchange("k_far", k0.at[5], k0.at[2], k0.at[18], k0.at[21])

    for level in range(LEVELS - 1):
        coarsen(level, K[level], K[level + 1], 1.0 / 16.0)
    exchange("k1", k1.at[pl.ds(4, 3)], k1.at[pl.ds(1, 3)], k1.at[pl.ds(9, 3)], k1.at[pl.ds(12, 3)])
    exchange("k2", k2.at[pl.ds(4, 3)], k2.at[pl.ds(1, 3)], k2.at[pl.ds(5, 3)], k2.at[pl.ds(8, 3)])
    exchange("k3", k3.at[pl.ds(5, 2)], k3.at[pl.ds(3, 2)], k3.at[pl.ds(5, 2)], k3.at[pl.ds(7, 2)])
    exchange("k3_2", k3.at[pl.ds(5, 2)], k3.at[pl.ds(1, 2)], k3.at[pl.ds(5, 2)], k3.at[pl.ds(9, 2)], 2)
    exchange("k3_3", k3.at[5], k3.at[0], k3.at[6], k3.at[11], 3)

    scales(0, 4, 20)
    relax(0, 5, 19, da0)
    update(0, 6, 18, da0)
    relax(0, 6, 18, db0)
    db0[3] = zero
    db0[20] = zero
    update(0, 7, 17, db0)
    scales(1, 4, 12)
    scales(2, 4, 8)
    scales(3, 5, 7)

    arrived("p", "k", "r")
    for side, edge, halo in ((0, 4, 3), (1, 19, 20)):
        r0[halo] = rh[side] + k0[halo] * p0[edge - 3]
        r0[edge] = r0[edge] + k0[edge] * ph[side]
        scales(0, halo, halo + 1)
    for lo, hi in ((3, 5), (19, 21)):
        relax(0, lo, hi, da0)
    for lo, hi in ((4, 6), (18, 20)):
        update(0, lo, hi, da0)
    for lo, hi in ((4, 6), (18, 20)):
        relax(0, lo, hi, db0)
    exchange("d", db0.at[4], dh.at[0], db0.at[19], dh.at[1])
    for lo, hi in ((4, 7), (17, 20)):
        update(0, lo, hi, db0)
    coarsen(0, r0, r1, 0.25)
    for n, i in enumerate((4, 5, 10, 11)):
        lr1[6 + n] = r1[i]
    for n, i in enumerate((4, 5, 18, 19)):
        lr0[4 + n] = r0[i]
    exchange("b1", lr1.at[pl.ds(6, 2)], r1.at[pl.ds(2, 2)], lr1.at[pl.ds(8, 2)], r1.at[pl.ds(12, 2)])
    exchange("r0", lr0.at[pl.ds(4, 2)], lr0.at[pl.ds(0, 2)], lr0.at[pl.ds(6, 2)], lr0.at[pl.ds(2, 2)])

    def gather(at):
        for i in at:
            c0[i - 4] = p0[i - 3] + da0[i] + db0[i]
    rows(4, 20, 2, gather)
    arrived("k_far", "k1", "k2", "k3", "k3_2", "k3_3")
    for lo, hi in ((2, 3), (21, 22)):
        scales(0, lo, hi)
    for lo, hi in ((1, 4), (12, 15)):
        scales(1, lo, hi)
    for lo, hi in ((1, 4), (8, 11)):
        scales(2, lo, hi)
    for lo, hi in ((0, 5), (7, 12)):
        scales(3, lo, hi)

    arrived("d", "b1")
    for side, edge, halo, edge1, halo1 in ((0, 4, 3, 4, 3), (1, 19, 20, 11, 12)):
        mine = k0[edge] * dh[side]
        theirs = k0[halo] * db0[edge]
        r0[edge] = r0[edge] + mine
        dh[4 + side] = theirs
        r1[edge1] = r1[edge1] + lanes(0.25 * mine, coarse0_ref[...])
        r1[halo1] = r1[halo1] + lanes(0.25 * theirs, coarse0_ref[...])

    relax(1, 2, 14, da1)
    update(1, 3, 13, da1)
    relax(1, 3, 13, db1)
    update(1, 4, 12, db1)
    coarsen(1, r1, r2, 0.25)
    exchange("b2", r2.at[pl.ds(4, 2)], lr2.at[pl.ds(6, 2)], r2.at[pl.ds(6, 2)], lr2.at[pl.ds(8, 2)])
    for i in range(4, 12):
        c1[i] = da1[i] + db1[i]
    exchange("r1", r1.at[pl.ds(4, 3)], lr1.at[pl.ds(0, 3)], r1.at[pl.ds(9, 3)], lr1.at[pl.ds(3, 3)])
    exchange("c1", c1.at[pl.ds(4, 2)], lc1.at[pl.ds(0, 2)], c1.at[pl.ds(10, 2)], lc1.at[pl.ds(2, 2)])

    arrived("r0")
    r0[2] = lr0[0]
    r0[3] = lr0[1] + dh[4]
    r0[20] = lr0[2] + dh[5]
    r0[21] = lr0[3]

    arrived("b2")
    sent("b2")
    for n, i in enumerate((2, 3, 8, 9)):
        r2[i] = lr2[6 + n]
    relax(2, 2, 10, da2)
    update(2, 3, 9, da2)
    relax(2, 3, 9, db2)
    update(2, 4, 8, db2)
    coarsen(2, r2, r3, 0.25)
    for n in range(2):
        lr2[10 + n] = r3[5 + n]
    b3 = lr2.at[pl.ds(10, 2)]
    exchange("b3", b3, r3.at[pl.ds(3, 2)], b3, r3.at[pl.ds(7, 2)])
    exchange("b3_2", b3, r3.at[pl.ds(1, 2)], b3, r3.at[pl.ds(9, 2)], 2)
    exchange("b3_3", lr2.at[10], r3.at[0], lr2.at[11], r3.at[11], 3)
    for i in range(4, 8):
        c2[i] = da2[i] + db2[i]
    exchange("r2", r2.at[pl.ds(4, 3)], lr2.at[pl.ds(0, 3)], r2.at[pl.ds(5, 3)], lr2.at[pl.ds(3, 3)])
    exchange("c2", c2.at[pl.ds(4, 2)], lc2.at[pl.ds(0, 2)], c2.at[pl.ds(6, 2)], lc2.at[pl.ds(2, 2)])

    arrived("b3", "b3_2", "b3_3")
    relax(3, 0, 12, da3)
    update(3, 1, 11, da3)
    relax(3, 1, 11, db3)
    update(3, 2, 10, db3)
    def first(at):
        for i in at:
            c3[i] = da3[i] + db3[i]
    rows(3, 9, 2, first)
    relax(3, 2, 10, da3)
    update(3, 3, 9, da3)
    relax(3, 3, 9, db3)
    def last(at):
        for i in at:
            c3[i] = c3[i] + da3[i] + db3[i]
    rows(3, 9, 2, last)

    refine(2, 3, 9, c3, e2, v2)
    arrived("r2", "c2")
    sent("r2", "c2")
    for n, i in enumerate((1, 2, 3, 8, 9, 10)):
        r2[i] = lr2[n]
    for n, i in enumerate((2, 3, 8, 9)):
        c2[i] = lc2[n]
    lift(2, 1, 11, e2, v2)
    relax(2, 1, 11, da2)
    update(2, 2, 10, da2)
    relax(2, 2, 10, db2)
    def sum2(at):
        for i in at:
            c2[i] = c2[i] + e2[i] + da2[i] + db2[i]
    rows(2, 10, 2, sum2)

    refine(1, 2, 10, c2, e1, v1)
    arrived("r1", "c1")
    sent("r1", "c1")
    for n, i in enumerate((1, 2, 3, 12, 13, 14)):
        r1[i] = lr1[n]
    for n, i in enumerate((2, 3, 12, 13)):
        c1[i] = lc1[n]
    lift(1, 1, 15, e1, v1)
    relax(1, 1, 15, da1)
    update(1, 2, 14, da1)
    relax(1, 2, 14, db1)
    def sum1(at):
        for i in at:
            c1[i] = c1[i] + e1[i] + da1[i] + db1[i]
    rows(2, 14, 2, sum1)

    refine(0, 2, 14, c1, e0, v0)
    sent("d")
    lift(0, 2, 22, e0, v0)
    relax(0, 2, 22, da0)
    update(0, 3, 21, da0)
    relax(0, 3, 21, db0)
    def sum0(at):
        for i in at:
            c0[i - 4] = c0[i - 4] + e0[i] + da0[i] + db0[i]
    rows(4, 20, 2, sum0)
    for i in range(16):
        pltpu.make_async_copy(c0.at[i], out_u.at[:, i, :], out_sem.at[0]).start()
    update(0, 4, 20, db0)
    for i in range(16):
        pltpu.make_async_copy(r0.at[4 + i], out_r.at[:, i, :], out_sem.at[1]).start()
    sent(*list(pending))
    pltpu.make_async_copy(c0, c0, out_sem.at[0]).wait()
    pltpu.make_async_copy(r0.at[pl.ds(4, 16)], r0.at[pl.ds(4, 16)], out_sem.at[1]).wait()


def solution(mesh):
    faces, tiles = mesh.shape["face"], mesh.shape["tile"]

    def field(count, width):
        return pltpu.VMEM((count, LEV, width), F32)

    def body(pressure, forcing, stiffness, vertical_op, col_inverse):
        out = jax.ShapeDtypeStruct(pressure.shape, F32)
        def level(n, extra):
            return [field(n, LANES)] * 8 + [field(m, LANES) for m in extra]
        scratch = (
            [field(18, 256)] + [field(24, 256)] * 7 + [field(2, 256)] * 2 + [field(6, 256), field(8, 256)]
            + level(16, (10, 4)) + level(12, (12, 4))
            + [field(12, LANES)] * 6 + [field(12, LANES), field(16, 256)]
            + [
                pltpu.VMEM((LEVELS, LEV, 3 * LEV), BF16),
                pltpu.VMEM((LEV, 3 * LEV), BF16),
                pltpu.VMEM((256, 128), BF16),
                pltpu.VMEM((512, 128), BF16),
                pltpu.VMEM((256, 128), BF16),
                pltpu.VMEM((256, 256), BF16),
                pltpu.SemaphoreType.DMA((3,)),
                pltpu.SemaphoreType.DMA((2,)),
                pltpu.SemaphoreType.DMA((len(MESSAGES), 2)),
                pltpu.SemaphoreType.DMA((len(MESSAGES), 2)),
            ]
        )
        return pl.pallas_call(
            functools.partial(kernel, faces, tiles),
            out_shape=(out, out),
            in_specs=[pl.BlockSpec(memory_space=pl.ANY)] * 3 + [pl.BlockSpec(memory_space=pltpu.VMEM)] * 2,
            out_specs=(pl.BlockSpec(memory_space=pl.ANY),) * 2,
            scratch_shapes=scratch,
            compiler_params=pltpu.CompilerParams(
                collective_id=0, has_side_effects=True, vmem_limit_bytes=48 * 1024 * 1024
            ),
            cost_estimate=pl.CostEstimate(flops=2_000_000_000, bytes_accessed=5_000_000, transcendentals=0),
        )(pressure, forcing, stiffness, vertical_op, col_inverse)

    belt = P(None, ("face", "tile"), None)
    return jax.shard_map(
        body,
        mesh=mesh,
        in_specs=(belt, belt, belt, P(), P()),
        out_specs=(belt, belt),
        check_vma=False,
    )
```

profile of v0, /device:TPU:32, one launch (start us, length us, event | category | flops | bytes accessed | tf_op | source)
XLA Modules:
  0.0 105.4 jit_solution(14951433498272576853)
XLA Ops:
  0.6 0.0 copy-start
  0.6 1.2 %copy-done = f32[64,16,256]{2,1,0:T(8,128)S(1)} copy-done((f32[64,16,256]{2,1,0:T(8,128)S(1)}, f32[64,16,256]{2,1,0:T(8,128)}, u32[]{:S(2)}) %copy-start) | copy-done | bytes 1048600
  1.9 0.0 copy-start.1
  1.9 1.2 %copy-done.1 = f32[64,16,256]{2,1,0:T(8,128)S(1)} copy-done((f32[64,16,256]{2,1,0:T(8,128)S(1)}, f32[64,16,256]{2,1,0:T(8,128)}, u32[]{:S(2)}) %copy-start.1) | copy-done | bytes 1048600
  3.1 0.0 copy-start.2
  3.1 1.2 %copy-done.2 = f32[64,16,256]{2,1,0:T(8,128)S(1)} copy-done((f32[64,16,256]{2,1,0:T(8,128)S(1)}, f32[64,16,256]{2,1,0:T(8,128)}, u32[]{:S(2)}) %copy-start.2) | copy-done | bytes 1048600
  4.3 0.0 copy-start.3
  4.3 0.9 copy-done.3
  5.2 0.0 copy-start.4
  5.2 0.8 copy-done.4
  6.0 97.5 %shard_map.68 = (f32[64,16,256]{2,1,0:T(8,128)S(1)}, f32[64,16,256]{2,1,0:T(8,128)S(1)}) custom-call(f32[64,16,256]{2,1,0:T(8,128)S(1)} %copy-done, f32[64,16,256]{2,1,0:T(8,128)S(1)} %copy-done.1, f32[64,16,256]{2,1,0:T(8,128)S(1)} %copy-done.2, f32[64,64]{1,0:T(8,128)S(1)} %copy-done.4, f32[4,64,64]{2,1,0:T(8,128)S(1)} %copy-done.3), custom_call_target="tpu_custom_call" | custom-call | flops 2000000000 | bytes 5000000 | tf_op jit(solution)/shard_map/pallas_call | solution.py:421
  103.4 1.0 copy.9
  104.4 1.0 copy.10
Async XLA Ops:
  0.6 1.2 %copy-start = (f32[64,16,256]{2,1,0:T(8,128)S(1)}, f32[64,16,256]{2,1,0:T(8,128)}, u32[]{:S(2)}) copy-start(f32[64,16,256]{2,1,0:T(8,128)} %p_hbm.1) | copy-start | bytes 3145732
  1.9 1.2 %copy-start.1 = (f32[64,16,256]{2,1,0:T(8,128)S(1)}, f32[64,16,256]{2,1,0:T(8,128)}, u32[]{:S(2)}) copy-start(f32[64,16,256]{2,1,0:T(8,128)} %f_hbm.1) | copy-start | bytes 3145732
  3.1 1.2 %copy-start.2 = (f32[64,16,256]{2,1,0:T(8,128)S(1)}, f32[64,16,256]{2,1,0:T(8,128)}, u32[]{:S(2)}) copy-start(f32[64,16,256]{2,1,0:T(8,128)} %k_hbm.1) | copy-start | bytes 3145732
  4.3 0.9 copy-start.3
  5.2 0.8 copy-start.4
where the time goes:
time: 106 us; the launch traced here: 105 us
  Pallas kernels  97.5 us (92%)
  local copies, waits for them, and re-layouts  7.27 us (7%)
    pallas_call x1, Pallas kernels, body(): pl.pallas_call(functools.partial(kernel, faces, tiles), out_shape=(out, o...  97.5 us
    unnamed x12, local copies, waits for them, and re-layouts  7.27 us

commit v1 on v0

--- a/solution.py
+++ b/solution.py
@@ -15,12 +15,13 @@
 F32, BF16 = jnp.float32, jnp.bfloat16
 MESH = pl.DeviceIdType.MESH
 LANES = 128
+VMEM_MIB = 62
 
 HALO = (4, 4, 4, 5)
 
 MESSAGES = (
     "p", "k", "r", "k_far", "k1", "k2", "k3", "k3_2", "k3_3", "d", "b1", "r0", "b2", "r1", "c1",
-    "b3", "b3_2", "b3_3", "r2", "c2",
+    "b3", "b3_2", "b3_3", "r2",
 )
 
 
@@ -57,8 +58,8 @@
     faces, tiles, p_hbm, f_hbm, k_hbm, vop_ref, inv_ref, out_u, out_r,
     p0, k0, s0, r0, da0, db0, e0, v0, ph, rh, dh, lr0,
     k1, s1, r1, da1, db1, c1, e1, v1, lr1, lc1,
-    k2, s2, r2, da2, db2, c2, e2, v2, lr2, lc2,
-    k3, s3, r3, da3, db3, c3, v3, c0,
+    k2, s2, r2, da2, db2, c2, e2, v2, lr2, lb2,
+    k3, s3, r3, da3, db3, c3, c0, lk2, q2, q3, lq3,
     w_ref, wv_ref, coarse_ref, coarse0_ref, fine_ref, fine0_ref,
     in_sem, out_sem, send_sem, recv_sem,
 ):
@@ -115,6 +116,40 @@
     def lanes(x, matrix):
         high, low = split(x)
         return jnp.dot(jnp.concatenate([high, low], axis=1), matrix, preferred_element_type=F32)
+
+    def lane_mask(x, lo, hi):
+        lane = lax.broadcasted_iota(jnp.int32, x.shape, 1)
+        return jnp.where((lane >= lo) & (lane < hi), x, 0.0)
+
+    def pack2(a, b):
+        return a + pltpu.roll(b, 64, 1)
+
+    def unpack2(x):
+        return lane_mask(x, 0, 64), lane_mask(pltpu.roll(x, 64, 1), 0, 64)
+
+    def pack3(a, b):
+        both = a + pltpu.roll(b, 32, 1)
+        half = LEV // 2
+        return both[:half] + pltpu.roll(both[half:], 64, 1)
+
+    def unpack3(x):
+        parts = [x] + [pltpu.roll(x, shift, 1) for shift in (64, 96, 32)]
+        parts = [lane_mask(part, 0, 32) for part in parts]
+        return jnp.concatenate(parts[:2], axis=0), jnp.concatenate(parts[2:], axis=0)
+
+    def spread3(name, at):
+        for distance in (1, 2, 3):
+            low, high = at * 6 + 3 - distance, at * 6 + 2 + distance
+            suffix = "" if distance == 1 else "_%d" % distance
+            exchange(name + suffix, q3.at[at], lq3.at[low], q3.at[at], lq3.at[high], distance)
+
+    def gather3(at, to):
+        for n, i in enumerate((-1, 1, 3, 7, 9, 11)):
+            first_row, second_row = unpack3(lq3[at * 6 + n])
+            if i >= 0:
+                to[i] = first_row
+            if i + 1 < 12:
+                to[i + 1] = second_row
 
     def masked(level):
         return level < 2
@@ -152,13 +187,13 @@
         def fn(at):
             for i in at:
                 S[level][i] = top / (damping + 4.0 * K[level][i])
-        rows(lo, hi, 2, fn)
+        rows(lo, hi, 24, fn)
 
     def relax(level, lo, hi, d_ref):
         def fn(at):
             for i in at:
                 d_ref[i] = columns(w_ref[level], S[level][i] * R[level][i])
-        rows(lo, hi, 4, fn)
+        rows(lo, hi, 24, fn)
 
     def update(level, lo, hi, d_ref):
         shift = nominal_stiff / 4.0**level
@@ -168,7 +203,7 @@
                 beside_sum = d_ref[i - 1] + d_ref[i + 1] + lateral(d, masked(level))
                 t = S[level][i] * R[level][i]
                 R[level][i] = R[level][i] - t + shift * d + K[level][i] * (beside_sum - 4.0 * d)
-        rows(lo, hi, 2, fn)
+        rows(lo, hi, 24, fn)
 
     def lift(level, lo, hi, e_ref, v_ref):
         def fn(at):
@@ -176,15 +211,15 @@
                 e = e_ref[i]
                 beside_sum = e_ref[i - 1] + e_ref[i + 1] + lateral(e, masked(level))
                 R[level][i] = R[level][i] - v_ref[i] + K[level][i] * (beside_sum - 4.0 * e)
-        rows(lo, hi, 2, fn)
-
-    def coarsen(level, src, dst, scale):
+        rows(lo, hi, 24, fn)
+
+    def coarsen(level, src, dst, scale, which=None):
         matrix = coarse0_ref if level == 0 else coarse_ref
         def fn(at):
             for j in at:
                 fine = H[level] + 2 * j
                 dst[H[level + 1] + j] = lanes(scale * (src[fine] + src[fine + 1]), matrix[...])
-        rows(0, own[level + 1], 2, fn)
+        fn(range(own[level + 1]) if which is None else which)
 
     def refine(level, lo, hi, src, e_ref, v_ref):
         matrix = fine0_ref if level == 0 else fine_ref
@@ -197,7 +232,7 @@
                 for i in (to, to + 1):
                     e_ref[i] = value
                     v_ref[i] = product
-        rows(lo, hi, 2, fn)
+        rows(lo, hi, 24, fn)
 
     zero = jnp.zeros((LEV, 256), F32)
     p0[0] = zero
@@ -211,7 +246,7 @@
             x = p0[i + 1]
             beside_sum = p0[i] + p0[i + 2] + lateral(x, True)
             r0[i + 4] = r0[i + 4] - columns(wv_ref[...], x) + k0[i + 4] * (beside_sum - 4.0 * x)
-    rows(0, 16, 2, start)
+    rows(0, 16, 24, start)
     dh[2] = r0[4]
     dh[3] = r0[19]
 
@@ -219,15 +254,14 @@
     exchange("p", p0.at[1], ph.at[0], p0.at[16], ph.at[1])
     exchange("k", k0.at[4], k0.at[3], k0.at[19], k0.at[20])
     exchange("r", dh.at[2], rh.at[0], dh.at[3], rh.at[1])
-    exchange("k_far", k0.at[5], k0.at[2], k0.at[18], k0.at[21])
 
     for level in range(LEVELS - 1):
         coarsen(level, K[level], K[level + 1], 1.0 / 16.0)
     exchange("k1", k1.at[pl.ds(4, 3)], k1.at[pl.ds(1, 3)], k1.at[pl.ds(9, 3)], k1.at[pl.ds(12, 3)])
-    exchange("k2", k2.at[pl.ds(4, 3)], k2.at[pl.ds(1, 3)], k2.at[pl.ds(5, 3)], k2.at[pl.ds(8, 3)])
-    exchange("k3", k3.at[pl.ds(5, 2)], k3.at[pl.ds(3, 2)], k3.at[pl.ds(5, 2)], k3.at[pl.ds(7, 2)])
-    exchange("k3_2", k3.at[pl.ds(5, 2)], k3.at[pl.ds(1, 2)], k3.at[pl.ds(5, 2)], k3.at[pl.ds(9, 2)], 2)
-    exchange("k3_3", k3.at[5], k3.at[0], k3.at[6], k3.at[11], 3)
+    q2[6] = pack2(k2[4], k2[5])
+    q2[7] = pack2(k2[6], k2[7])
+    exchange("k2", q2.at[pl.ds(6, 2)], lk2.at[pl.ds(0, 2)], q2.at[pl.ds(6, 2)], lk2.at[pl.ds(2, 2)])
+    q3[0] = pack3(k3[5], k3[6])
 
     scales(0, 4, 20)
     relax(0, 5, 19, da0)
@@ -236,6 +270,7 @@
     db0[3] = zero
     db0[20] = zero
     update(0, 7, 17, db0)
+    coarsen(0, r0, r1, 0.25, (2, 3, 4, 5))
     scales(1, 4, 12)
     scales(2, 4, 8)
     scales(3, 5, 7)
@@ -254,7 +289,7 @@
     exchange("d", db0.at[4], dh.at[0], db0.at[19], dh.at[1])
     for lo, hi in ((4, 7), (17, 20)):
         update(0, lo, hi, db0)
-    coarsen(0, r0, r1, 0.25)
+    coarsen(0, r0, r1, 0.25, (0, 1, 6, 7))
     for n, i in enumerate((4, 5, 10, 11)):
         lr1[6 + n] = r1[i]
     for n, i in enumerate((4, 5, 18, 19)):
@@ -262,19 +297,19 @@
     exchange("b1", lr1.at[pl.ds(6, 2)], r1.at[pl.ds(2, 2)], lr1.at[pl.ds(8, 2)], r1.at[pl.ds(12, 2)])
     exchange("r0", lr0.at[pl.ds(4, 2)], lr0.at[pl.ds(0, 2)], lr0.at[pl.ds(6, 2)], lr0.at[pl.ds(2, 2)])
 
+    spread3("k3", 0)
+
     def gather(at):
         for i in at:
             c0[i - 4] = p0[i - 3] + da0[i] + db0[i]
-    rows(4, 20, 2, gather)
-    arrived("k_far", "k1", "k2", "k3", "k3_2", "k3_3")
-    for lo, hi in ((2, 3), (21, 22)):
-        scales(0, lo, hi)
+    rows(4, 20, 24, gather)
+    arrived("k1", "k2")
+    for n in range(4):
+        k2[(0, 2, 8, 10)[n]], k2[(1, 3, 9, 11)[n]] = unpack2(lk2[n])
     for lo, hi in ((1, 4), (12, 15)):
         scales(1, lo, hi)
     for lo, hi in ((1, 4), (8, 11)):
         scales(2, lo, hi)
-    for lo, hi in ((0, 5), (7, 12)):
-        scales(3, lo, hi)
 
     arrived("d", "b1")
     for side, edge, halo, edge1, halo1 in ((0, 4, 3, 4, 3), (1, 19, 20, 11, 12)):
@@ -290,11 +325,15 @@
     relax(1, 3, 13, db1)
     update(1, 4, 12, db1)
     coarsen(1, r1, r2, 0.25)
-    exchange("b2", r2.at[pl.ds(4, 2)], lr2.at[pl.ds(6, 2)], r2.at[pl.ds(6, 2)], lr2.at[pl.ds(8, 2)])
+    q2[4] = pack2(r2[4], r2[5])
+    q2[5] = pack2(r2[6], r2[7])
+    exchange("b2", q2.at[4], lb2.at[0], q2.at[5], lb2.at[1])
     for i in range(4, 12):
         c1[i] = da1[i] + db1[i]
     exchange("r1", r1.at[pl.ds(4, 3)], lr1.at[pl.ds(0, 3)], r1.at[pl.ds(9, 3)], lr1.at[pl.ds(3, 3)])
     exchange("c1", c1.at[pl.ds(4, 2)], lc1.at[pl.ds(0, 2)], c1.at[pl.ds(10, 2)], lc1.at[pl.ds(2, 2)])
+
+    exchange("k_far", k0.at[5], k0.at[2], k0.at[18], k0.at[21])
 
     arrived("r0")
     r0[2] = lr0[0]
@@ -303,26 +342,29 @@
     r0[21] = lr0[3]
 
     arrived("b2")
-    sent("b2")
-    for n, i in enumerate((2, 3, 8, 9)):
-        r2[i] = lr2[6 + n]
+    r2[2], r2[3] = unpack2(lb2[0])
+    r2[8], r2[9] = unpack2(lb2[1])
     relax(2, 2, 10, da2)
     update(2, 3, 9, da2)
     relax(2, 3, 9, db2)
     update(2, 4, 8, db2)
     coarsen(2, r2, r3, 0.25)
-    for n in range(2):
-        lr2[10 + n] = r3[5 + n]
-    b3 = lr2.at[pl.ds(10, 2)]
-    exchange("b3", b3, r3.at[pl.ds(3, 2)], b3, r3.at[pl.ds(7, 2)])
-    exchange("b3_2", b3, r3.at[pl.ds(1, 2)], b3, r3.at[pl.ds(9, 2)], 2)
-    exchange("b3_3", lr2.at[10], r3.at[0], lr2.at[11], r3.at[11], 3)
+    q3[1] = pack3(r3[5], r3[6])
+    spread3("b3", 1)
     for i in range(4, 8):
         c2[i] = da2[i] + db2[i]
-    exchange("r2", r2.at[pl.ds(4, 3)], lr2.at[pl.ds(0, 3)], r2.at[pl.ds(5, 3)], lr2.at[pl.ds(3, 3)])
-    exchange("c2", c2.at[pl.ds(4, 2)], lc2.at[pl.ds(0, 2)], c2.at[pl.ds(6, 2)], lc2.at[pl.ds(2, 2)])
+    q2[0] = pack2(c2[4], c2[5])
+    q2[1] = pack2(r2[4], r2[5])
+    q2[2] = pack2(r2[6], r2[7])
+    q2[3] = pack2(c2[6], c2[7])
+    exchange("r2", q2.at[pl.ds(0, 3)], lr2.at[pl.ds(0, 3)], q2.at[pl.ds(1, 3)], lr2.at[pl.ds(3, 3)])
+    arrived("k3", "k3_2", "k3_3")
+    gather3(0, k3)
+    for lo, hi in ((0, 5), (7, 12)):
+        scales(3, lo, hi)
 
     arrived("b3", "b3_2", "b3_3")
+    gather3(1, r3)
     relax(3, 0, 12, da3)
     update(3, 1, 11, da3)
     relax(3, 1, 11, db3)
@@ -330,22 +372,22 @@
     def first(at):
         for i in at:
             c3[i] = da3[i] + db3[i]
-    rows(3, 9, 2, first)
+    rows(3, 9, 24, first)
     relax(3, 2, 10, da3)
     update(3, 3, 9, da3)
     relax(3, 3, 9, db3)
     def last(at):
         for i in at:
             c3[i] = c3[i] + da3[i] + db3[i]
-    rows(3, 9, 2, last)
+    rows(3, 9, 24, last)
 
     refine(2, 3, 9, c3, e2, v2)
-    arrived("r2", "c2")
-    sent("r2", "c2")
-    for n, i in enumerate((1, 2, 3, 8, 9, 10)):
-        r2[i] = lr2[n]
-    for n, i in enumerate((2, 3, 8, 9)):
-        c2[i] = lc2[n]
+    arrived("r2")
+    for n in range(2):
+        r2[2 * n], r2[2 * n + 1] = unpack2(lr2[n])
+        r2[2 * n + 8], r2[2 * n + 9] = unpack2(lr2[4 + n])
+    c2[2], c2[3] = unpack2(lr2[2])
+    c2[8], c2[9] = unpack2(lr2[3])
     lift(2, 1, 11, e2, v2)
     relax(2, 1, 11, da2)
     update(2, 2, 10, da2)
@@ -353,7 +395,7 @@
     def sum2(at):
         for i in at:
             c2[i] = c2[i] + e2[i] + da2[i] + db2[i]
-    rows(2, 10, 2, sum2)
+    rows(2, 10, 24, sum2)
 
     refine(1, 2, 10, c2, e1, v1)
     arrived("r1", "c1")
@@ -369,8 +411,11 @@
     def sum1(at):
         for i in at:
             c1[i] = c1[i] + e1[i] + da1[i] + db1[i]
-    rows(2, 14, 2, sum1)
-
+    rows(2, 14, 24, sum1)
+
+    arrived("k_far")
+    for lo, hi in ((2, 3), (21, 22)):
+        scales(0, lo, hi)
     refine(0, 2, 14, c1, e0, v0)
     sent("d")
     lift(0, 2, 22, e0, v0)
@@ -380,7 +425,7 @@
     def sum0(at):
         for i in at:
             c0[i - 4] = c0[i - 4] + e0[i] + da0[i] + db0[i]
-    rows(4, 20, 2, sum0)
+    rows(4, 20, 24, sum0)
     for i in range(16):
         pltpu.make_async_copy(c0.at[i], out_u.at[:, i, :], out_sem.at[0]).start()
     update(0, 4, 20, db0)
@@ -403,8 +448,9 @@
             return [field(n, LANES)] * 8 + [field(m, LANES) for m in extra]
         scratch = (
             [field(18, 256)] + [field(24, 256)] * 7 + [field(2, 256)] * 2 + [field(6, 256), field(8, 256)]
-            + level(16, (10, 4)) + level(12, (12, 4))
-            + [field(12, LANES)] * 6 + [field(12, LANES), field(16, 256)]
+            + level(16, (10, 4)) + level(12, (6, 2))
+            + [field(12, LANES)] * 6 + [field(16, 256), field(4, LANES), field(8, LANES)]
+            + [pltpu.VMEM((2, LEV // 2, LANES), F32), pltpu.VMEM((12, LEV // 2, LANES), F32)]
             + [
                 pltpu.VMEM((LEVELS, LEV, 3 * LEV), BF16),
                 pltpu.VMEM((LEV, 3 * LEV), BF16),
@@ -425,7 +471,7 @@
             out_specs=(pl.BlockSpec(memory_space=pl.ANY),) * 2,
             scratch_shapes=scratch,
             compiler_params=pltpu.CompilerParams(
-                collective_id=0, has_side_effects=True, vmem_limit_bytes=48 * 1024 * 1024
+                collective_id=0, has_side_effects=True, vmem_limit_bytes=VMEM_MIB * 1024 * 1024
             ),
             cost_estimate=pl.CostEstimate(flops=2_000_000_000, bytes_accessed=5_000_000, transcendentals=0),
         )(pressure, forcing, stiffness, vertical_op, col_inverse)

time: 106 us -> 76.6 us (0.72)
  Pallas kernels: 97.5 us -> 71.3 us
  local copies, waits for them, and re-layouts: 7.27 us -> 3.32 us
    pallas_call x1, Pallas kernels: 97.5 us -> 71.3 us  [body(): pl.pallas_call(functools.partial(kernel, faces, tiles), out_shape=(out, o...]
    unnamed x12 -> x4, local copies, waits for them, and re-layouts: 7.27 us -> 3.32 us
where the time goes in v1:
time: 76.6 us; the launch traced here: 75.3 us
  Pallas kernels  71.3 us (93%)
  local copies, waits for them, and re-layouts  3.32 us (4%)
    pallas_call x1, Pallas kernels, body(): pl.pallas_call(functools.partial(kernel, faces, tiles), out_shape=(out, o...  71.3 us
    unnamed x4, local copies, waits for them, and re-layouts  3.32 us

profile of v1, /device:TPU:32, one launch (start us, length us, event | category | flops | bytes accessed | tf_op | source)
XLA Modules:
  0.0 75.3 jit_solution(7124383863352831304)
XLA Ops:
  0.6 71.3 %shard_map.68 = (f32[64,16,256]{2,1,0:T(8,128)}, f32[64,16,256]{2,1,0:T(8,128)}) custom-call(f32[64,16,256]{2,1,0:T(8,128)} %p_hbm.1, f32[64,16,256]{2,1,0:T(8,128)} %f_hbm.1, f32[64,16,256]{2,1,0:T(8,128)} %k_hbm.1, f32[64,64]{1,0:T(8,128)} %vop_ref.1, f32[4,64,64]{2,1,0:T(8,128)} %inv_ref.1), custom_call_target="tpu_custom_call" | custom-call | flops 2000000000 | bytes 5000000 | tf_op jit(solution)/shard_map/pallas_call | solution.py:467
  71.9 0.0 copy-start
  71.9 2.4 %copy.9 = f32[64,16,256]{2,1,0:T(8,128)} copy(f32[64,16,256]{2,1,0:T(8,128)} %get-tuple-element.4) | data formatting | bytes 2097152
  74.3 0.0 copy-done
  74.3 1.0 %copy.10 = f32[64,16,256]{2,1,0:T(8,128)} copy(f32[64,16,256]{2,1,0:T(8,128)S(1)} %copy-done) | data formatting | bytes 2097152
Async XLA Ops:
  71.9 2.4 %copy-start = (f32[64,16,256]{2,1,0:T(8,128)S(1)}, f32[64,16,256]{2,1,0:T(8,128)}, u32[]{:S(2)}) copy-start(f32[64,16,256]{2,1,0:T(8,128)} %get-tuple-element.5) | copy-start | bytes 3145732

commit v2 on v1

--- a/solution.py
+++ b/solution.py
@@ -59,7 +59,7 @@
     p0, k0, s0, r0, da0, db0, e0, v0, ph, rh, dh, lr0,
     k1, s1, r1, da1, db1, c1, e1, v1, lr1, lc1,
     k2, s2, r2, da2, db2, c2, e2, v2, lr2, lb2,
-    k3, s3, r3, da3, db3, c3, c0, lk2, q2, q3, lq3,
+    k3, s3, r3, da3, db3, c3, c0, lk2, q2, q3, lq3, q4,
     w_ref, wv_ref, coarse_ref, coarse0_ref, fine_ref, fine0_ref,
     in_sem, out_sem, send_sem, recv_sem,
 ):
@@ -137,19 +137,31 @@
         parts = [lane_mask(part, 0, 32) for part in parts]
         return jnp.concatenate(parts[:2], axis=0), jnp.concatenate(parts[2:], axis=0)
 
-    def spread3(name, at):
-        for distance in (1, 2, 3):
+    def pack4(x):
+        quarter = LEV // 4
+        parts = [x[n * quarter : (n + 1) * quarter] for n in range(4)]
+        return sum(pltpu.roll(part, 32 * n, 1) for n, part in enumerate(parts[1:], 1)) + parts[0]
+
+    def unpack4(x):
+        parts = [x] + [pltpu.roll(x, LANES - 32 * n, 1) for n in (1, 2, 3)]
+        return jnp.concatenate([lane_mask(part, 0, 32) for part in parts], axis=0)
+
+    def spread3(name, at, src):
+        q3[at] = pack3(src[5], src[6])
+        q4[2 * at] = pack4(src[5])
+        q4[2 * at + 1] = pack4(src[6])
+        for distance in (1, 2):
             low, high = at * 6 + 3 - distance, at * 6 + 2 + distance
             suffix = "" if distance == 1 else "_%d" % distance
             exchange(name + suffix, q3.at[at], lq3.at[low], q3.at[at], lq3.at[high], distance)
+        first_in, last_in = 4 + 2 * at, 5 + 2 * at
+        exchange(name + "_3", q4.at[2 * at], q4.at[first_in], q4.at[2 * at + 1], q4.at[last_in], 3)
 
     def gather3(at, to):
-        for n, i in enumerate((-1, 1, 3, 7, 9, 11)):
-            first_row, second_row = unpack3(lq3[at * 6 + n])
-            if i >= 0:
-                to[i] = first_row
-            if i + 1 < 12:
-                to[i + 1] = second_row
+        for n, i in ((1, 1), (2, 3), (3, 7), (4, 9)):
+            to[i], to[i + 1] = unpack3(lq3[at * 6 + n])
+        to[0] = unpack4(q4[4 + 2 * at])
+        to[11] = unpack4(q4[5 + 2 * at])
 
     def masked(level):
         return level < 2
@@ -261,7 +273,6 @@
     q2[6] = pack2(k2[4], k2[5])
     q2[7] = pack2(k2[6], k2[7])
     exchange("k2", q2.at[pl.ds(6, 2)], lk2.at[pl.ds(0, 2)], q2.at[pl.ds(6, 2)], lk2.at[pl.ds(2, 2)])
-    q3[0] = pack3(k3[5], k3[6])
 
     scales(0, 4, 20)
     relax(0, 5, 19, da0)
@@ -297,7 +308,7 @@
     exchange("b1", lr1.at[pl.ds(6, 2)], r1.at[pl.ds(2, 2)], lr1.at[pl.ds(8, 2)], r1.at[pl.ds(12, 2)])
     exchange("r0", lr0.at[pl.ds(4, 2)], lr0.at[pl.ds(0, 2)], lr0.at[pl.ds(6, 2)], lr0.at[pl.ds(2, 2)])
 
-    spread3("k3", 0)
+    spread3("k3", 0, k3)
 
     def gather(at):
         for i in at:
@@ -328,10 +339,12 @@
     q2[4] = pack2(r2[4], r2[5])
     q2[5] = pack2(r2[6], r2[7])
     exchange("b2", q2.at[4], lb2.at[0], q2.at[5], lb2.at[1])
-    for i in range(4, 12):
+    for n, i in enumerate((5, 10)):
+        lc1[2 + n] = db1[i]
+    exchange("c1", lc1.at[2], lc1.at[0], lc1.at[3], lc1.at[1])
+    exchange("r1", r1.at[pl.ds(5, 2)], lr1.at[pl.ds(0, 2)], r1.at[pl.ds(9, 2)], lr1.at[pl.ds(2, 2)])
+    for i in range(3, 13):
         c1[i] = da1[i] + db1[i]
-    exchange("r1", r1.at[pl.ds(4, 3)], lr1.at[pl.ds(0, 3)], r1.at[pl.ds(9, 3)], lr1.at[pl.ds(3, 3)])
-    exchange("c1", c1.at[pl.ds(4, 2)], lc1.at[pl.ds(0, 2)], c1.at[pl.ds(10, 2)], lc1.at[pl.ds(2, 2)])
 
     exchange("k_far", k0.at[5], k0.at[2], k0.at[18], k0.at[21])
 
@@ -349,15 +362,12 @@
     relax(2, 3, 9, db2)
     update(2, 4, 8, db2)
     coarsen(2, r2, r3, 0.25)
-    q3[1] = pack3(r3[5], r3[6])
-    spread3("b3", 1)
-    for i in range(4, 8):
+    spread3("b3", 1, r3)
+    q2[0] = pack2(r2[5], r2[6])
+    q2[1] = pack2(db2[5], db2[6])
+    exchange("r2", q2.at[pl.ds(0, 2)], lr2.at[pl.ds(0, 2)], q2.at[pl.ds(0, 2)], lr2.at[pl.ds(2, 2)])
+    for i in range(3, 9):
         c2[i] = da2[i] + db2[i]
-    q2[0] = pack2(c2[4], c2[5])
-    q2[1] = pack2(r2[4], r2[5])
-    q2[2] = pack2(r2[6], r2[7])
-    q2[3] = pack2(c2[6], c2[7])
-    exchange("r2", q2.at[pl.ds(0, 3)], lr2.at[pl.ds(0, 3)], q2.at[pl.ds(1, 3)], lr2.at[pl.ds(3, 3)])
     arrived("k3", "k3_2", "k3_3")
     gather3(0, k3)
     for lo, hi in ((0, 5), (7, 12)):
@@ -383,11 +393,14 @@
 
     refine(2, 3, 9, c3, e2, v2)
     arrived("r2")
-    for n in range(2):
-        r2[2 * n], r2[2 * n + 1] = unpack2(lr2[n])
-        r2[2 * n + 8], r2[2 * n + 9] = unpack2(lr2[4 + n])
-    c2[2], c2[3] = unpack2(lr2[2])
-    c2[8], c2[9] = unpack2(lr2[3])
+    db2[2] = unpack2(lr2[1])[1]
+    db2[9] = unpack2(lr2[3])[0]
+    update(2, 3, 4, db2)
+    update(2, 8, 9, db2)
+    r2[1], r2[2] = unpack2(lr2[0])
+    r2[9], r2[10] = unpack2(lr2[2])
+    for i in (2, 9):
+        c2[i] = da2[i] + db2[i]
     lift(2, 1, 11, e2, v2)
     relax(2, 1, 11, da2)
     update(2, 2, 10, da2)
@@ -400,10 +413,14 @@
     refine(1, 2, 10, c2, e1, v1)
     arrived("r1", "c1")
     sent("r1", "c1")
-    for n, i in enumerate((1, 2, 3, 12, 13, 14)):
+    for n, i in enumerate((2, 13)):
+        db1[i] = lc1[n]
+    update(1, 3, 4, db1)
+    update(1, 12, 13, db1)
+    for n, i in enumerate((1, 2, 13, 14)):
         r1[i] = lr1[n]
-    for n, i in enumerate((2, 3, 12, 13)):
-        c1[i] = lc1[n]
+    for n, i in enumerate((2, 13)):
+        c1[i] = da1[i] + lc1[n]
     lift(1, 1, 15, e1, v1)
     relax(1, 1, 15, da1)
     update(1, 2, 14, da1)
@@ -451,6 +468,7 @@
             + level(16, (10, 4)) + level(12, (6, 2))
             + [field(12, LANES)] * 6 + [field(16, 256), field(4, LANES), field(8, LANES)]
             + [pltpu.VMEM((2, LEV // 2, LANES), F32), pltpu.VMEM((12, LEV // 2, LANES), F32)]
+            + [pltpu.VMEM((8, LEV // 4, LANES), F32)]
             + [
                 pltpu.VMEM((LEVELS, LEV, 3 * LEV), BF16),
                 pltpu.VMEM((LEV, 3 * LEV), BF16),

time: 76.6 us -> 73.2 us (0.956)
  the two profiles are of different devices: /device:TPU:32 before, /device:TPU:2 now
where the time goes in v2:
time: 73.2 us; the launch traced here: 73 us
  Pallas kernels  69 us (94%)
  local copies, waits for them, and re-layouts  3.32 us (5%)
    pallas_call x1, Pallas kernels, body(): pl.pallas_call(functools.partial(kernel, faces, tiles), out_shape=(out, o...  69 us
    unnamed x4, local copies, waits for them, and re-layouts  3.32 us

profile of v2, /device:TPU:2, one launch (start us, length us, event | category | flops | bytes accessed | tf_op | source)
XLA Modules:
  0.0 73.0 jit_solution(4011519215328978163)
XLA Ops:
  0.6 69.0 %shard_map.68 = (f32[64,16,256]{2,1,0:T(8,128)}, f32[64,16,256]{2,1,0:T(8,128)}) custom-call(f32[64,16,256]{2,1,0:T(8,128)} %p_hbm.1, f32[64,16,256]{2,1,0:T(8,128)} %f_hbm.1, f32[64,16,256]{2,1,0:T(8,128)} %k_hbm.1, f32[64,64]{1,0:T(8,128)} %vop_ref.1, f32[4,64,64]{2,1,0:T(8,128)} %inv_ref.1), custom_call_target="tpu_custom_call" | custom-call | flops 2000000000 | bytes 5000000 | tf_op jit(solution)/shard_map/pallas_call | solution.py:485
  69.6 0.0 copy-start
  69.6 2.4 %copy.9 = f32[64,16,256]{2,1,0:T(8,128)} copy(f32[64,16,256]{2,1,0:T(8,128)} %get-tuple-element.4) | data formatting | bytes 2097152
  72.0 0.0 copy-done
  72.0 1.0 %copy.10 = f32[64,16,256]{2,1,0:T(8,128)} copy(f32[64,16,256]{2,1,0:T(8,128)S(1)} %copy-done) | data formatting | bytes 2097152
Async XLA Ops:
  69.6 2.4 %copy-start = (f32[64,16,256]{2,1,0:T(8,128)S(1)}, f32[64,16,256]{2,1,0:T(8,128)}, u32[]{:S(2)}) copy-start(f32[64,16,256]{2,1,0:T(8,128)} %get-tuple-element.5) | copy-start | bytes 3145732

commit v3 on v2

--- a/solution.py
+++ b/solution.py
@@ -346,7 +346,6 @@
     for i in range(3, 13):
         c1[i] = da1[i] + db1[i]
 
-    exchange("k_far", k0.at[5], k0.at[2], k0.at[18], k0.at[21])
 
     arrived("r0")
     r0[2] = lr0[0]
@@ -366,6 +365,7 @@
     q2[0] = pack2(r2[5], r2[6])
     q2[1] = pack2(db2[5], db2[6])
     exchange("r2", q2.at[pl.ds(0, 2)], lr2.at[pl.ds(0, 2)], q2.at[pl.ds(0, 2)], lr2.at[pl.ds(2, 2)])
+    exchange("k_far", k0.at[5], k0.at[2], k0.at[18], k0.at[21])
     for i in range(3, 9):
         c2[i] = da2[i] + db2[i]
     arrived("k3", "k3_2", "k3_3")

time: 73.2 us -> 75.3 us (1.029)
  the two profiles are of different devices: /device:TPU:2 before, /device:TPU:32 now
where the time goes in v3:
time: 75.3 us; the launch traced here: 75.1 us
  Pallas kernels  71.1 us (94%)
  local copies, waits for them, and re-layouts  3.32 us (4%)
    pallas_call x1, Pallas kernels, body(): pl.pallas_call(functools.partial(kernel, faces, tiles), out_shape=(out, o...  71.1 us
    unnamed x4, local copies, waits for them, and re-layouts  3.32 us

profile of v3, /device:TPU:32, one launch (start us, length us, event | category | flops | bytes accessed | tf_op | source)
XLA Modules:
  0.0 75.1 jit_solution(13425081016355394975)
XLA Ops:
  0.6 71.1 %shard_map.68 = (f32[64,16,256]{2,1,0:T(8,128)}, f32[64,16,256]{2,1,0:T(8,128)}) custom-call(f32[64,16,256]{2,1,0:T(8,128)} %p_hbm.1, f32[64,16,256]{2,1,0:T(8,128)} %f_hbm.1, f32[64,16,256]{2,1,0:T(8,128)} %k_hbm.1, f32[64,64]{1,0:T(8,128)} %vop_ref.1, f32[4,64,64]{2,1,0:T(8,128)} %inv_ref.1), custom_call_target="tpu_custom_call" | custom-call | flops 2000000000 | bytes 5000000 | tf_op jit(solution)/shard_map/pallas_call | solution.py:485
  71.7 0.0 copy-start
  71.8 2.4 %copy.9 = f32[64,16,256]{2,1,0:T(8,128)} copy(f32[64,16,256]{2,1,0:T(8,128)} %get-tuple-element.4) | data formatting | bytes 2097152
  74.1 0.0 copy-done
  74.1 1.0 %copy.10 = f32[64,16,256]{2,1,0:T(8,128)} copy(f32[64,16,256]{2,1,0:T(8,128)S(1)} %copy-done) | data formatting | bytes 2097152
Async XLA Ops:
  71.7 2.4 %copy-start = (f32[64,16,256]{2,1,0:T(8,128)S(1)}, f32[64,16,256]{2,1,0:T(8,128)}, u32[]{:S(2)}) copy-start(f32[64,16,256]{2,1,0:T(8,128)} %get-tuple-element.5) | copy-start | bytes 3145732
